TPU v7x, 32 devices: a whole 2x2x4 slice. The times are simulated.
32 devices in a mesh: groups: 2 (over x), kvp: 16 (over z, y, core).
Axes of the slice: x: 2, y: 2, z: 4, core: 2. Of those that a mesh axis runs over, the one named last changes fastest.
Arguments:
- queries: bfloat16 [512, 4096], P(('groups', 'kvp')), parts along dimension 0, may hold values from -8 to 8
- rotated_span_keys: bfloat16 [512, 512], P(('groups', 'kvp')), parts along dimension 0, may hold values from -8 to 8
- incoming_values: bfloat16 [512, 512], P(('groups', 'kvp')), parts along dimension 0, may hold values from -6 to 6
- stored_keys: bfloat16 [32768, 512], P(('groups', 'kvp')), parts along dimension 0, may hold values from -8 to 8
- stored_values: bfloat16 [32768, 512], P(('groups', 'kvp')), parts along dimension 0, may hold values from -6 to 6
- shard_lens: int32 [32], P('groups'), parts along dimension 0, may hold values from 1 to 1024, 12288 in all
- span_starts: int32 [4], P('groups'), parts along dimension 0, may hold values from 6144 to 12288
Outputs:
- attended: bfloat16 [512, 4096], P(('groups', 'kvp')), parts along dimension 0
There are 2 independent parts, one for each index of `groups`. A program takes and returns all parts, laid end to end along the dimension named above; each array names one. Nothing has to cross between parts.
Inputs may be any that keep to these rules, and one draw needn't show every extreme that they name: `shard_lens`: the lengths of the 16 shards sum to 12288; one shard is full.
All inputs are finite; a program needn't handle non-finite values.
Results may differ from a plain program's by a relative error of at most 0.0023.
Values may be sent and summed in bfloat16 or wider, within the bound.
A program may use at most 64 MiB of HBM per device.

v0:
```python
import jax
import jax.numpy as jnp
from jax import lax
from jax.sharding import PartitionSpec as P

QUERY_HEADS = 32
KEY_VALUE_HEADS = 4
HEAD_SIZE = 128
SPAN = 128
SPANS = 2


NEG_LARGE = -1e30


def softmax_part(query_rows, per_head_keys, per_head_values, visible, scale):
    scores = (
        jnp.einsum("rhgd,khd->rhgk", query_rows, per_head_keys, preferred_element_type=jnp.float32)
        * scale
    )
    visible_mask = visible[:, None, None, :]
    maxima = jnp.max(jnp.where(visible_mask, scores, NEG_LARGE), axis=-1)
    weights = jnp.where(visible_mask, jnp.exp(scores - maxima[..., None]), 0.0)
    totals = jnp.sum(weights, axis=-1)
    numerators = jnp.einsum(
        "rhgk,khd->rhgd",
        weights.astype(jnp.bfloat16),
        per_head_values,
        preferred_element_type=jnp.float32,
    )
    return (numerators, maxima, totals)


def shards(
    queries, rotated_span_keys, incoming_values, stored_keys, stored_values, shard_lens, span_starts
):
    shard_count = lax.axis_size("kvp")
    device = lax.axis_index("kvp")
    device_local_rows = queries.shape[0]
    cache_slot_count = stored_keys.shape[0]
    query_group_size = QUERY_HEADS // KEY_VALUE_HEADS
    scale = HEAD_SIZE ** (-0.5)
    offsets = jnp.cumsum(shard_lens) - shard_lens
    device_pick = (jnp.arange(shard_count, dtype=jnp.int32) == device).astype(jnp.int32)
    my_start = jnp.sum(offsets * device_pick)
    my_length = jnp.sum(shard_lens * device_pick)
    slot_index = jnp.arange(cache_slot_count, dtype=jnp.int32)
    positions = my_start + slot_index
    live_slots = slot_index < my_length
    per_head_keys = stored_keys.reshape(cache_slot_count, KEY_VALUE_HEADS, HEAD_SIZE)
    per_head_values = stored_values.reshape(cache_slot_count, KEY_VALUE_HEADS, HEAD_SIZE)
    span_index = jnp.arange(SPANS, dtype=jnp.int32)
    every_query = lax.all_gather(queries, "kvp", axis=0, tiled=True)
    overall_rows = every_query.shape[0]
    block_row_range = 64

    def one_block(first):
        rows_here = lax.dynamic_slice_in_dim(every_query, first, block_row_range, 0).reshape(
            block_row_range, KEY_VALUE_HEADS, query_group_size, HEAD_SIZE
        )
        row_ids = first + jnp.arange(block_row_range, dtype=jnp.int32)
        compare = (row_ids // SPAN)[:, None] == span_index[None, :]
        limits = jnp.sum(jnp.where(compare, span_starts[None, :], 0), axis=1)
        visible = live_slots[None, :] & (positions[None, :] < limits[:, None])
        numerators, maxima, totals = softmax_part(
            rows_here, per_head_keys, per_head_values, visible, scale
        )
        return (
            numerators.reshape(block_row_range, QUERY_HEADS * HEAD_SIZE),
            maxima.reshape(block_row_range, QUERY_HEADS),
            totals.reshape(block_row_range, QUERY_HEADS),
        )

    block_starts = jnp.arange(overall_rows // block_row_range, dtype=jnp.int32) * block_row_range
    numerators, maxima, totals = lax.map(one_block, block_starts)
    numerators = numerators.reshape(overall_rows, QUERY_HEADS * HEAD_SIZE)
    maxima = maxima.reshape(overall_rows, QUERY_HEADS)
    totals = totals.reshape(overall_rows, QUERY_HEADS)
    span_key_rows, span_value_rows = (
        lax.all_gather(rotated_span_keys, "kvp", axis=0, tiled=True),
        lax.all_gather(incoming_values, "kvp", axis=0, tiled=True),
    )
    own_ids = device * device_local_rows + jnp.arange(device_local_rows, dtype=jnp.int32)
    key_ids = jnp.arange(overall_rows, dtype=jnp.int32)
    span_visible = (key_ids[None, :] // SPAN == own_ids[:, None] // SPAN) & (
        key_ids[None, :] <= own_ids[:, None]
    )
    local_query = queries.reshape(device_local_rows, KEY_VALUE_HEADS, query_group_size, HEAD_SIZE)
    span_num, span_max, span_total = softmax_part(
        local_query,
        span_key_rows.reshape(overall_rows, KEY_VALUE_HEADS, HEAD_SIZE),
        span_value_rows.reshape(overall_rows, KEY_VALUE_HEADS, HEAD_SIZE),
        span_visible,
        scale,
    )
    span_num = span_num.reshape(device_local_rows, QUERY_HEADS, HEAD_SIZE)
    span_max = span_max.reshape(device_local_rows, QUERY_HEADS)
    span_total = span_total.reshape(device_local_rows, QUERY_HEADS)
    arrived_num, arrived_max, arrived_total = (
        lax.all_to_all(
            numerators.reshape(shard_count, device_local_rows, QUERY_HEADS * HEAD_SIZE),
            "kvp",
            split_axis=0,
            concat_axis=0,
            tiled=True,
        ),
        lax.all_to_all(
            maxima.reshape(shard_count, device_local_rows, QUERY_HEADS),
            "kvp",
            split_axis=0,
            concat_axis=0,
            tiled=True,
        ),
        lax.all_to_all(
            totals.reshape(shard_count, device_local_rows, QUERY_HEADS),
            "kvp",
            split_axis=0,
            concat_axis=0,
            tiled=True,
        ),
    )
    own_max = jnp.max(arrived_max, axis=0)
    factor = jnp.exp(arrived_max - own_max[None])
    summed_num = jnp.sum(
        arrived_num.reshape(shard_count, device_local_rows, QUERY_HEADS, HEAD_SIZE)
        * factor[..., None],
        axis=0,
    )
    summed_total = jnp.sum(arrived_total * factor, axis=0)
    overall = jnp.maximum(own_max, span_max)
    shard_factor = jnp.exp(own_max - overall)
    span_factor = jnp.exp(span_max - overall)
    numerator = summed_num * shard_factor[..., None] + span_num * span_factor[..., None]
    denominator = summed_total * shard_factor + span_total * span_factor
    return (
        (numerator / denominator[..., None])
        .reshape(device_local_rows, QUERY_HEADS * HEAD_SIZE)
        .astype(jnp.bfloat16)
    )


def solution(mesh):
    in_specs = (
        P(("groups", "kvp"), None),
        P(("groups", "kvp"), None),
        P(("groups", "kvp"), None),
        P(("groups", "kvp"), None),
        P(("groups", "kvp"), None),
        P("groups"),
        P("groups"),
    )
    out_specs = P(("groups", "kvp"), None)
    return jax.shard_map(shards, mesh=mesh, in_specs=in_specs, out_specs=out_specs, check_vma=False)
```

profile of v0, /device:TPU:11, one launch (start us, length us, event | category | flops | bytes accessed | tf_op | source)
XLA Modules:
  0.0 303.4 jit_solution(7402948748695958223)
XLA Ops:
  6.5 0.7 all-gather.2.cloned.1.call-update
  7.3 0.7 copy.122
  8.2 1.5 copy.120
  10.3 1.5 copy.121
  11.8 1.3 copy.124
  13.2 0.7 fusion.35
  13.9 37.7 %all-gather.2.cloned.1.call-done = bf16[256,4096]{1,0:T(8,128)(2,1)} async-done(((bf16[16,4096]{1,0:T(8,128)(2,1)}), bf16[256,4096]{1,0:T(8,128)(2,1)}) %all-gather.2.cloned.1.call-update) | async-done | bytes 2097168 | tf_op jit(solution)/shard_map/all_gather | solution.py:53
  51.6 81.5 %while.17 = (s32[]{:T(128)}, f32[4,64,4096]{2,1,0:T(8,128)}, f32[4,64,32]{1,2,0:T(8,128)S(1)}, f32[4,64,32]{1,2,0:T(8,128)S(1)}, s32[4]{0:T(128)S(1)}, /*index=5...) while((s32[]{:T(128)}, f32[4,64,4096]{2,1,0:T(8,128)}, ...), condition=%wide.region_7.8_spmd.clone, body=%wide.region_3.7_spmd.clone.sunk | while | flops 1096940800 | bytes 71184104 | solution.py:75
  54.3 1.2 dynamic-slice_bitcast_fusion.2
  55.6 0.7 and_select_fusion.4
  57.8 1.9 fusion.49
  59.7 3.2 %copy-done = f32[4,64,8,1024]{3,2,1,0:T(8,128)} copy-done((f32[4,64,8,1024]{3,2,1,0:T(8,128)}, f32[4,64,8,1024]{3,2,1,0:T(8,128)S(1)}, u32[]{:S(2)}) %copy-start) | copy-done | bytes 8388632 | tf_op jit(solution)/shard_map/while
  63.0 2.5 fusion.51
  65.7 4.8 %fusion.50 = f32[64,4,8,128]{3,2,0,1:T(8,128)S(1)} fusion(f32[4,64,8,1024]{3,2,1,0:T(8,128)} %copy-done, f32[64,4,8]{2,0,1:T(8,128)S(1)} %get-tuple-element.365, pred[64,1024]{1,0:T(8,128)(4,1)S(1)} %compare_and_fusion.2, bf16[1024,4,128]{2,0,1:T(8,128)(2,1)} %get-tuple-element.404), kind=kOutput, calls=%fused_computation.12.clone.1 | convolution fusion | flops 545259520 | bytes 10559488 | tf_op jit(solution)/shard_map/while/body/eval_jaxpr/rhgk,khd->rhgd/dot_general | solution.py:25
  70.8 1.2 constant_dynamic-update-slice_fusion.2
  74.7 1.2 dynamic-slice_bitcast_fusion.2
  76.1 0.7 and_select_fusion.4
  78.3 1.9 fusion.49
  80.2 3.2 %copy-done = f32[4,64,8,1024]{3,2,1,0:T(8,128)} copy-done((f32[4,64,8,1024]{3,2,1,0:T(8,128)}, f32[4,64,8,1024]{3,2,1,0:T(8,128)S(1)}, u32[]{:S(2)}) %copy-start) | copy-done | bytes 8388632 | tf_op jit(solution)/shard_map/while
  83.4 2.5 fusion.51
  86.1 4.8 %fusion.50 = f32[64,4,8,128]{3,2,0,1:T(8,128)S(1)} fusion(f32[4,64,8,1024]{3,2,1,0:T(8,128)} %copy-done, f32[64,4,8]{2,0,1:T(8,128)S(1)} %get-tuple-element.365, pred[64,1024]{1,0:T(8,128)(4,1)S(1)} %compare_and_fusion.2, bf16[1024,4,128]{2,0,1:T(8,128)(2,1)} %get-tuple-element.404), kind=kOutput, calls=%fused_computation.12.clone.1 | convolution fusion | flops 545259520 | bytes 10559488 | tf_op jit(solution)/shard_map/while/body/eval_jaxpr/rhgk,khd->rhgd/dot_general | solution.py:25
  91.3 1.1 constant_dynamic-update-slice_fusion.2
  95.1 1.2 dynamic-slice_bitcast_fusion.2
  98.6 1.9 fusion.49
  100.5 3.2 %copy-done = f32[4,64,8,1024]{3,2,1,0:T(8,128)} copy-done((f32[4,64,8,1024]{3,2,1,0:T(8,128)}, f32[4,64,8,1024]{3,2,1,0:T(8,128)S(1)}, u32[]{:S(2)}) %copy-start) | copy-done | bytes 8388632 | tf_op jit(solution)/shard_map/while
  103.7 2.5 fusion.51
  106.4 4.8 %fusion.50 = f32[64,4,8,128]{3,2,0,1:T(8,128)S(1)} fusion(f32[4,64,8,1024]{3,2,1,0:T(8,128)} %copy-done, f32[64,4,8]{2,0,1:T(8,128)S(1)} %get-tuple-element.365, pred[64,1024]{1,0:T(8,128)(4,1)S(1)} %compare_and_fusion.2, bf16[1024,4,128]{2,0,1:T(8,128)(2,1)} %get-tuple-element.404), kind=kOutput, calls=%fused_computation.12.clone.1 | convolution fusion | flops 545259520 | bytes 10559488 | tf_op jit(solution)/shard_map/while/body/eval_jaxpr/rhgk,khd->rhgd/dot_general | solution.py:25
  111.6 1.1 constant_dynamic-update-slice_fusion.2
  115.4 1.2 dynamic-slice_bitcast_fusion.2
  116.7 0.7 and_select_fusion.4
  118.9 1.9 fusion.49
  120.9 3.2 %copy-done = f32[4,64,8,1024]{3,2,1,0:T(8,128)} copy-done((f32[4,64,8,1024]{3,2,1,0:T(8,128)}, f32[4,64,8,1024]{3,2,1,0:T(8,128)S(1)}, u32[]{:S(2)}) %copy-start) | copy-done | bytes 8388632 | tf_op jit(solution)/shard_map/while
  124.1 2.5 fusion.51
  126.8 4.8 %fusion.50 = f32[64,4,8,128]{3,2,0,1:T(8,128)S(1)} fusion(f32[4,64,8,1024]{3,2,1,0:T(8,128)} %copy-done, f32[64,4,8]{2,0,1:T(8,128)S(1)} %get-tuple-element.365, pred[64,1024]{1,0:T(8,128)(4,1)S(1)} %compare_and_fusion.2, bf16[1024,4,128]{2,0,1:T(8,128)(2,1)} %get-tuple-element.404), kind=kOutput, calls=%fused_computation.12.clone.1 | convolution fusion | flops 545259520 | bytes 10559488 | tf_op jit(solution)/shard_map/while/body/eval_jaxpr/rhgk,khd->rhgd/dot_general | solution.py:25
  132.0 1.1 constant_dynamic-update-slice_fusion.2
  133.1 0.7 reshape.300
  133.9 4.8 %all-to-all-start.1 = ((f32[16,1,512]{2,1,0:T(1,128)}), f32[16,1,512]{2,1,0:T(1,128)S(1)}, u32[]{:S(2)}, u32[]{:S(2)}) async-start(f32[16,1,512]{2,1,0:T(1,128)} %reshape.300), calls=%async_computation.1 | async-start | bytes 65536 | tf_op jit(solution)/shard_map/all_to_all | solution.py:107
  138.9 4.8 %all-to-all-done.1 = f32[16,1,512]{2,1,0:T(1,128)S(1)} async-done(((f32[16,1,512]{2,1,0:T(1,128)}), f32[16,1,512]{2,1,0:T(1,128)S(1)}, u32[]{:S(2)}, u32[]{:S(2)}) %all-to-all-start.1) | async-done | bytes 32800 | tf_op jit(solution)/shard_map/all_to_all | solution.py:107
  143.7 9.2 %all_to_all.15 = f32[16,1,512]{2,1,0:T(1,128)S(1)} all-to-all(f32[16,1,512]{2,1,0:T(1,128)S(1)} %reshape.302), channel_id=1, replica_groups=mesh['groups'=2,'kvp'=16] {'kvp'}, dimensions={0} | all-to-all | bytes 65536 | tf_op jit(solution)/shard_map/all_to_all | solution.py:114
  152.8 6.0 %all-to-all-start = ((f32[16,16,4096]{2,1,0:T(8,128)}), f32[16,16,4096]{2,1,0:T(8,128)}, u32[]{:S(2)}, u32[]{:S(2)}) async-start(f32[16,16,4096]{2,1,0:T(8,128)} %bitcast.112), calls=%async_computation | async-start | bytes 8388608 | tf_op jit(solution)/shard_map/all_to_all | solution.py:100
  158.8 103.7 %all_gather.10 = bf16[256,512]{1,0:T(8,128)(2,1)S(1)} all-gather(bf16[16,512]{1,0:T(8,128)(2,1)S(1)} %copy-done.2), channel_id=1, replica_groups=mesh['groups'=2,'kvp'=16] {'kvp'}, dimensions={0}, use_global_device_ids=true | all-gather | bytes 278528 | tf_op jit(solution)/shard_map/all_gather | solution.py:80
  263.6 17.3 %all_gather.11 = bf16[256,512]{1,0:T(8,128)(2,1)S(1)} all-gather(bf16[16,512]{1,0:T(8,128)(2,1)S(1)} %copy-done.3), channel_id=1, replica_groups=mesh['groups'=2,'kvp'=16] {'kvp'}, dimensions={0}, use_global_device_ids=true | all-gather | bytes 278528 | tf_op jit(solution)/shard_map/all_gather | solution.py:81
  281.7 0.7 reduce.3
  282.6 0.7 reduce.2
  283.5 2.6 mul.83
  286.0 5.0 %mul.84 = f32[16,16,4096]{2,1,0:T(8,128)} reshape(f32[16,16,32,128]{3,2,1,0:T(8,128)} %mul.83) | data formatting | bytes 8388608 | tf_op jit(solution)/shard_map/mul | solution.py:125
  291.0 3.9 %multiply_reduce_fusion = f32[16,4096]{1,0:T(8,128)S(1)} fusion(f32[16,16,4096]{2,1,0:T(8,128)} %all-to-all-done, f32[16,16,4096]{2,1,0:T(8,128)} %mul.84), kind=kLoop, calls=%fused_computation.32 | loop fusion | flops 2031616 | bytes 8650752 | tf_op jit(solution)/shard_map/reduce_sum | solution.py:124
  295.3 1.2 fusion.27
  (92 shorter events, 15.2 us)
Async XLA Ops:
  6.5 6.6 %copy-start.4 = (s32[16]{0:T(128)S(1)}, s32[16]{0:T(128)}, u32[]{:S(2)}) copy-start(s32[16]{0:T(128)} %param.14) | copy-start | bytes 196
  6.5 45.0 %copy-start.5 = (s32[2]{0:T(128)S(1)}, s32[2]{0:T(128)}, u32[]{:S(2)}) copy-start(s32[2]{0:T(128)} %param.15) | copy-start | bytes 28
  6.5 45.0 %all-gather.2.cloned.1.call-start = ((), (), s32[]{:S(2)}) async-start(), calls=%async_computation.3 | async-start | bytes 2228224 | tf_op jit(solution)/shard_map/all_gather | solution.py:53
  59.7 3.2 %copy-start = (f32[4,64,8,1024]{3,2,1,0:T(8,128)}, f32[4,64,8,1024]{3,2,1,0:T(8,128)S(1)}, u32[]{:S(2)}) copy-start(f32[4,64,8,1024]{3,2,1,0:T(8,128)S(1)} %get-tuple-element.364) | copy-start | bytes 25165828 | tf_op jit(solution)/shard_map/while
  80.2 3.2 %copy-start = (f32[4,64,8,1024]{3,2,1,0:T(8,128)}, f32[4,64,8,1024]{3,2,1,0:T(8,128)S(1)}, u32[]{:S(2)}) copy-start(f32[4,64,8,1024]{3,2,1,0:T(8,128)S(1)} %get-tuple-element.364) | copy-start | bytes 25165828 | tf_op jit(solution)/shard_map/while
  100.5 3.2 %copy-start = (f32[4,64,8,1024]{3,2,1,0:T(8,128)}, f32[4,64,8,1024]{3,2,1,0:T(8,128)S(1)}, u32[]{:S(2)}) copy-start(f32[4,64,8,1024]{3,2,1,0:T(8,128)S(1)} %get-tuple-element.364) | copy-start | bytes 25165828 | tf_op jit(solution)/shard_map/while
  120.8 3.2 %copy-start = (f32[4,64,8,1024]{3,2,1,0:T(8,128)}, f32[4,64,8,1024]{3,2,1,0:T(8,128)S(1)}, u32[]{:S(2)}) copy-start(f32[4,64,8,1024]{3,2,1,0:T(8,128)S(1)} %get-tuple-element.364) | copy-start | bytes 25165828 | tf_op jit(solution)/shard_map/while
  133.0 25.8 %copy-start.2 = (bf16[16,512]{1,0:T(8,128)(2,1)S(1)}, bf16[16,512]{1,0:T(8,128)(2,1)}, u32[]{:S(2)}) copy-start(bf16[16,512]{1,0:T(8,128)(2,1)} %param.10) | copy-start | bytes 49156
  133.0 129.7 %copy-start.1 = (bf16[16,4096]{1,0:T(8,128)(2,1)S(1)}, bf16[16,4096]{1,0:T(8,128)(2,1)}, u32[]{:S(2)}) copy-start(bf16[16,4096]{1,0:T(8,128)(2,1)} %param.9) | copy-start | bytes 393220
  133.0 130.5 %copy-start.3 = (bf16[16,512]{1,0:T(8,128)(2,1)S(1)}, bf16[16,512]{1,0:T(8,128)(2,1)}, u32[]{:S(2)}) copy-start(bf16[16,512]{1,0:T(8,128)(2,1)} %param.11) | copy-start | bytes 49156
  133.9 9.8 %all-to-all-start.1 = ((f32[16,1,512]{2,1,0:T(1,128)}), f32[16,1,512]{2,1,0:T(1,128)S(1)}, u32[]{:S(2)}, u32[]{:S(2)}) async-start(f32[16,1,512]{2,1,0:T(1,128)} %reshape.300), calls=%async_computation.1 | async-start | bytes 65536 | tf_op jit(solution)/shard_map/all_to_all | solution.py:107
  152.8 138.2 %all-to-all-start = ((f32[16,16,4096]{2,1,0:T(8,128)}), f32[16,16,4096]{2,1,0:T(8,128)}, u32[]{:S(2)}, u32[]{:S(2)}) async-start(f32[16,16,4096]{2,1,0:T(8,128)} %bitcast.112), calls=%async_computation | async-start | bytes 8388608 | tf_op jit(solution)/shard_map/all_to_all | solution.py:100
Sparse Core Ops, SparseCore 0:
  9.5 41.9 all-gather.1
where the time goes:
time: 308 us; the launch traced here: 303 us
  blocking collectives  130 us (42%)
  waiting for transfers between devices  43.2 us (14%)
  local copies, waits for them, and re-layouts  42.8 us (14%)
  matrix products  27.5 us (9%)
  other arithmetic  26.7 us (9%)
  between operations  13.6 us (4%)
  starting transfers between devices  10.8 us (4%)
  loops' own time  8.62 us (3%)
    all_gather x1, blocking collectives, shards(): lax.all_gather(rotated_span_keys, 'kvp', axis=0, tiled=True)  104 us
    all_gather x1, waiting for transfers between devices, shards(): every_query = lax.all_gather(queries, 'kvp', axis=0, tiled=True)  37.7 us
    dot_general x5, matrix products, softmax_part(): jnp.einsum('rhgk,khd->rhgd', weights.astype(jnp.bfloat16), per_head_value...  19.6 us
    while x16, local copies, waits for them, and re-layouts  18.1 us
    all_gather x1, blocking collectives, shards(): lax.all_gather(incoming_values, 'kvp', axis=0, tiled=True)  17.3 us
    reduce_sum x4, other arithmetic, softmax_part(): totals = jnp.sum(weights, axis=-1)  10.1 us
    all_to_all x1, blocking collectives, shards(): lax.all_to_all(totals.reshape(shard_count, device_local_rows, QUERY_HEADS...  9.19 us
    another operation x1, loops' own time, shards(): numerators, maxima, totals = lax.map(one_block, block_starts)  8.62 us
  transfers between devices with their start and end apart: 3, of which 2 were waited for; matrix products, arithmetic and copies ran while one was open for 6% of the time, Pallas kernels for 0%

commit v1 on v0

v1 whole, which is shorter than its diff:
```python
import functools

import jax
import jax.numpy as jnp
from jax import lax
from jax.experimental import pallas as pl
from jax.experimental.pallas import tpu as pltpu
from jax.sharding import PartitionSpec as P

QUERY_HEADS = 32
HEADS = 4
GROUP = QUERY_HEADS // HEADS
HEAD_SIZE = 128
SPAN = 128
SPANS = 2
NEG = -1e30
SCALE2 = HEAD_SIZE ** (-0.5) * 1.4426950408889634
F32 = jnp.float32
BF16 = jnp.bfloat16
MESH = pl.DeviceIdType.MESH


def log2(x):
    return x.bit_length() - 1


def weigh(scores, visible):
    masked = jnp.where(visible, scores, NEG)
    top = jnp.max(masked, axis=0, keepdims=True)
    weights = jnp.exp2(masked * SCALE2 - top * SCALE2)
    return weights.astype(BF16), top * SCALE2, jnp.sum(weights, axis=0, keepdims=True)


def dot_nt(a, b):
    return lax.dot_general(a, b, (((1,), (1,)), ((), ())), preferred_element_type=F32)


def dot_nn(a, b):
    return lax.dot_general(a, b, (((1,), (0,)), ((), ())), preferred_element_type=F32)


def merge(one, two):
    num1, top1, sum1 = one
    num2, top2, sum2 = two
    top = jnp.maximum(top1, top2)
    f1, f2 = jnp.exp2(top1 - top), jnp.exp2(top2 - top)
    return num1 * f1 + num2 * f2, top, sum1 * f1 + sum2 * f2


def kernel(
    n, rows, pad, tile,
    counts, q_in, s_in, k_in, v_in, out,
    qbuf, sbuf, kbuf, vbuf, vt, svt, acc, rbuf, obuf,
    q_send, q_recv, s_send, s_recv, k_send, k_recv, v_send, v_recv, a_send, a_recv, o_send, o_recv,
):
    group = lax.axis_index("groups")
    me = lax.axis_index("kvp")
    head = lax.rem(me, HEADS)
    quad = lax.div(me, HEADS)
    quads = n // HEADS
    block = GROUP * rows
    per_quad = HEADS * block
    tiles = per_quad // tile
    slots = kbuf.shape[1]

    barrier = pltpu.get_barrier_semaphore()

    def greet(k, c):
        pl.semaphore_signal(barrier, inc=1, device_id=(group, lax.rem(me + k, n)), device_id_type=MESH)
        return c

    lax.fori_loop(1, n, greet, 0)
    pl.semaphore_wait(barrier, n - 1)

    def q_copy(k):
        to = lax.rem(me + k, n)
        return pltpu.make_async_remote_copy(
            src_ref=q_in.at[lax.rem(to, HEADS)],
            dst_ref=qbuf.at[pl.ds(pl.multiple_of(me * block, block), block)],
            send_sem=q_send.at[k], recv_sem=q_recv.at[k],
            device_id=(group, to), device_id_type=MESH,
        )

    def s_copy(k):
        to = lax.rem(me + k, n)
        return pltpu.make_async_remote_copy(
            src_ref=s_in.at[lax.rem(to, HEADS)],
            dst_ref=sbuf.at[:, pl.ds(pl.multiple_of(me * pad, pad), pad)],
            send_sem=s_send.at[k], recv_sem=s_recv.at[k],
            device_id=(group, to), device_id_type=MESH,
        )

    partner = head + 1 - 2 * lax.rem(head, 2)
    order = (head, partner, lax.rem(head + 2, HEADS), lax.rem(partner + 2, HEADS))

    def kv_copies(i):
        columns = pl.ds(pl.multiple_of(order[i] * HEAD_SIZE, HEAD_SIZE), HEAD_SIZE)
        if i == 0:
            return (
                pltpu.make_async_copy(k_in.at[:, columns], kbuf.at[0], k_recv.at[0]),
                pltpu.make_async_copy(v_in.at[:, columns], vbuf.at[0], v_recv.at[0]),
            )
        return tuple(
            pltpu.make_async_remote_copy(
                src_ref=src.at[:, columns], dst_ref=dst.at[i],
                send_sem=send.at[i], recv_sem=recv.at[i],
                device_id=(group, quad * HEADS + order[i]), device_id_type=MESH,
            )
            for src, dst, send, recv in ((k_in, kbuf, k_send, k_recv), (v_in, vbuf, v_send, v_recv))
        )

    kv = [kv_copies(i) for i in range(HEADS)]

    def send_q(k, c):
        q_copy(k).start()
        return c

    lax.fori_loop(1, n, send_q, 0)
    for i in range(HEADS):
        for copy in kv[i]:
            copy.start()

    def send_s(k, c):
        s_copy(k).start()
        return c

    lax.fori_loop(1, n, send_s, 0)
    qbuf[pl.ds(pl.multiple_of(me * block, block), block), :] = q_in[head]
    sbuf[:, pl.ds(pl.multiple_of(me * pad, pad), pad), :] = s_in[head]

    def wait_q(k, c):
        q_copy(k).wait_recv()
        return c

    lax.fori_loop(1, n, wait_q, 0)

    def wait_kv(i):
        for copy in kv[i]:
            if i == 0:
                copy.wait()
            else:
                copy.wait_recv()
        vt[i] = jnp.transpose(vbuf[i])

    slot_ids = lax.broadcasted_iota(jnp.int32, (slots, tile), 0)
    stat_ids = lax.broadcasted_iota(jnp.int32, (8, tile), 0)

    def queries_of(b):
        return qbuf[pl.ds(pl.multiple_of(b * tile, tile), tile), :]

    def part(i, b):
        count = counts[quad * HEADS + order[i], lax.div(b * tile, GROUP * SPAN)]
        weights, top, total = weigh(dot_nt(kbuf[i], queries_of(b)), slot_ids < count)
        return dot_nn(vt[i], weights), top, total

    def load(ref, *at):
        return (
            ref[(*at, slice(0, HEAD_SIZE))],
            ref[(*at, slice(HEAD_SIZE, HEAD_SIZE + 1))],
            ref[(*at, slice(HEAD_SIZE + 4, HEAD_SIZE + 5))],
        )

    def store(b, state):
        num, top, total = state
        acc[b, 0:HEAD_SIZE] = num
        acc[b, HEAD_SIZE : HEAD_SIZE + 8] = jnp.where(stat_ids < 4, top, total)

    wait_kv(0)

    def first(b, c):
        store(b, part(0, b))
        return c

    lax.fori_loop(0, quads * tiles, first, 0)
    wait_kv(1)

    def second(b, c):
        store(b, merge(load(acc, b), part(1, b)))
        return c

    lax.fori_loop(0, quads * tiles, second, 0)
    wait_kv(2)
    wait_kv(3)

    def a_copy(k):
        to = lax.rem(quad + k, quads)
        return pltpu.make_async_remote_copy(
            src_ref=acc.at[pl.ds(to * tiles, tiles)], dst_ref=rbuf.at[k],
            send_sem=a_send.at[k], recv_sem=a_recv.at[k],
            device_id=(group, to * HEADS + head), device_id_type=MESH,
        )

    def finish(to):
        def one(t, c):
            b = to * tiles + t
            state = merge(load(acc, b), part(2, b))
            store(b, merge(state, part(3, b)))
            return c

        lax.fori_loop(0, tiles, one, 0)

    def finish_and_send(k, c):
        finish(lax.rem(quad + k, quads))
        a_copy(k).start()
        return c

    lax.fori_loop(1, quads, finish_and_send, 0)
    finish(quad)

    def wait_s(k, c):
        s_copy(k).wait_recv()
        return c

    lax.fori_loop(1, n, wait_s, 0)
    svt[...] = jnp.transpose(sbuf[1])
    keys = n * pad
    key_ids = lax.broadcasted_iota(jnp.int32, (keys, tile), 0)
    key_rows = (key_ids >> log2(pad)) * rows + (key_ids & (pad - 1))
    key_live = (key_ids & (pad - 1)) < rows
    lane_ids = lax.broadcasted_iota(jnp.int32, (keys, tile), 1)

    def span(t, c):
        b = quad * tiles + t
        ids = lane_ids + b * tile
        q_rows = (ids >> log2(block)) * rows + (ids & (rows - 1))
        visible = key_live & (key_rows >> log2(SPAN) == q_rows >> log2(SPAN)) & (key_rows <= q_rows)
        weights, top, total = weigh(dot_nt(sbuf[0], queries_of(b)), visible)
        store(b, merge(load(acc, b), (dot_nn(svt[...], weights), top, total)))
        return c

    lax.fori_loop(0, tiles, span, 0)

    def gather(k, c):
        a_copy(k).wait_recv()

        def one(t, c2):
            b = quad * tiles + t
            store(b, merge(load(acc, b), load(rbuf, k, t)))
            return c2

        lax.fori_loop(0, tiles, one, 0)
        return c

    lax.fori_loop(1, quads, gather, 0)

    def normal(t, c):
        num, top, total = load(acc, quad * tiles + t)
        obuf[pl.ds(pl.multiple_of(t * tile, tile), tile), :] = jnp.transpose(num / total).astype(BF16)
        return c

    lax.fori_loop(0, tiles, normal, 0)

    def o_copy(i):
        return pltpu.make_async_remote_copy(
            src_ref=obuf.at[pl.ds(pl.multiple_of(order[i] * block, block), block)], dst_ref=out.at[head],
            send_sem=o_send.at[i], recv_sem=o_recv.at[i],
            device_id=(group, quad * HEADS + order[i]), device_id_type=MESH,
        )

    for i in range(1, HEADS):
        o_copy(i).start()
    out[head] = obuf[pl.ds(pl.multiple_of(head * block, block), block), :]
    for i in range(1, HEADS):
        pltpu.make_async_remote_copy(
            src_ref=obuf.at[pl.ds(0, block)], dst_ref=out.at[order[i]],
            send_sem=o_send.at[i], recv_sem=o_recv.at[i],
            device_id=(group, quad * HEADS + order[i]), device_id_type=MESH,
        ).wait_recv()
    for i in range(1, HEADS):
        o_copy(i).wait_send()
        for copy in kv[i]:
            copy.wait_send()

    def drain(k, c):
        q_copy(k).wait_send()
        s_copy(k).wait_send()
        return c

    lax.fori_loop(1, n, drain, 0)

    def drain_a(k, c):
        a_copy(k).wait_send()
        return c

    lax.fori_loop(1, quads, drain_a, 0)


def shards(queries, span_keys, span_values, stored_keys, stored_values, shard_lens, span_starts):
    n = lax.axis_size("kvp")
    rows = queries.shape[0]
    slots = stored_keys.shape[0]
    pad = max(rows, 16)
    block = GROUP * rows
    quads = n // HEADS
    tile = min(256, HEADS * block)
    tiles = HEADS * block // tile
    ids = jnp.arange(n, dtype=jnp.int32)
    offsets = jnp.sum(jnp.where(ids[None, :] < ids[:, None], shard_lens[None, :], 0), axis=1)
    counts = jnp.minimum(shard_lens[:, None], span_starts[None, :] - offsets[:, None])
    q = queries.reshape(rows, QUERY_HEADS, HEAD_SIZE).transpose(1, 0, 2).reshape(HEADS, block, HEAD_SIZE)
    both = jnp.stack([span_keys, span_values]).reshape(2, rows, HEADS, HEAD_SIZE).transpose(2, 0, 1, 3)
    both = jnp.pad(both, ((0, 0), (0, 0), (0, pad - rows), (0, 0)))
    vmem = pl.BlockSpec(memory_space=pltpu.VMEM)
    dma = pltpu.SemaphoreType.DMA
    out = pl.pallas_call(
        functools.partial(kernel, n, rows, pad, tile),
        out_shape=jax.ShapeDtypeStruct((HEADS, block, HEAD_SIZE), BF16),
        in_specs=[
            pl.BlockSpec(memory_space=pltpu.SMEM), vmem, vmem,
            pl.BlockSpec(memory_space=pl.ANY), pl.BlockSpec(memory_space=pl.ANY),
        ],
        out_specs=vmem,
        scratch_shapes=[
            pltpu.VMEM((n * block, HEAD_SIZE), BF16),
            pltpu.VMEM((2, n * pad, HEAD_SIZE), BF16),
            pltpu.VMEM((HEADS, slots, HEAD_SIZE), BF16),
            pltpu.VMEM((HEADS, slots, HEAD_SIZE), BF16),
            pltpu.VMEM((HEADS, HEAD_SIZE, slots), BF16),
            pltpu.VMEM((HEAD_SIZE, n * pad), BF16),
            pltpu.VMEM((quads * tiles, HEAD_SIZE + 8, tile), F32),
            pltpu.VMEM((quads, tiles, HEAD_SIZE + 8, tile), F32),
            pltpu.VMEM((HEADS * block, HEAD_SIZE), BF16),
            dma((n,)), dma((n,)), dma((n,)), dma((n,)),
            dma((HEADS,)), dma((HEADS,)), dma((HEADS,)), dma((HEADS,)),
            dma((quads,)), dma((quads,)), dma((HEADS,)), dma((HEADS,)),
        ],
        compiler_params=pltpu.CompilerParams(
            collective_id=0, has_side_effects=True, vmem_limit_bytes=48 * 1024 * 1024
        ),
        name="spanned_attention",
    )(counts, q, both, stored_keys, stored_values)
    return out.reshape(QUERY_HEADS, rows, HEAD_SIZE).transpose(1, 0, 2).reshape(rows, QUERY_HEADS * HEAD_SIZE)


def solution(mesh):
    row = P(("groups", "kvp"), None)
    in_specs = (row, row, row, row, row, P("groups"), P("groups"))
    return jax.shard_map(shards, mesh=mesh, in_specs=in_specs, out_specs=row, check_vma=False)
```

time: 308 us -> 74.5 us (0.24); the launches traced: 303 us -> 74.2 us
  blocking collectives: 130 us -> 0 us
  Pallas kernels: 0 us -> 68.6 us
  waiting for transfers between devices: 43.2 us -> 0 us
  local copies, waits for them, and re-layouts: 42.8 us -> 4.6 us
  matrix products: 27.5 us -> 0 us
  other arithmetic: 26.7 us -> 0.92 us
  between operations: 13.6 us -> 0.07 us
  starting transfers between devices: 10.8 us -> 0 us
  loops' own time: 8.62 us -> 0 us
    all_gather x2 -> x0, blocking collectives: 121 us -> none  [the longest x1 104 us: shards(): lax.all_gather(rotated_span_keys, 'kvp', axis=0, tiled=True)]
    pallas_call x0 -> x1, Pallas kernels: none -> 68.6 us  [shards(): pl.pallas_call(functools.partial(kernel, n, rows, pad, tile), out_shape=j...]
    all_gather x1 -> x0, waiting for transfers between devices: 37.7 us -> none  [shards(): every_query = lax.all_gather(queries, 'kvp', axis=0, tiled=True)]
    dot_general x10 -> x0, matrix products: 27.5 us -> none  [the longest x5 19.6 us: softmax_part(): jnp.einsum('rhgk,khd->rhgd', weights.astype(jnp.bfloat16), per_head_value...]
    while x18 -> x0, local copies, waits for them, and re-layouts: 18.3 us -> none
    reduce_sum x11 -> x1, other arithmetic: 15.1 us -> 0.83 us  [shards(): jnp.sum(jnp.where(ids[None, :] < ids[:, None], shard_lens[None, :], 0), a...]
    all_to_all x2 -> x0, starting transfers between devices: 10.8 us -> none  [the longest x1 6 us: shards(): lax.all_to_all(numerators.reshape(shard_count, device_local_rows, QUERY_H...]
    all_to_all x1 -> x0, blocking collectives: 9.19 us -> none  [shards(): lax.all_to_all(totals.reshape(shard_count, device_local_rows, QUERY_HEADS...]
  transfers between devices with their start and end apart: 3 -> 0, of which waited for: 2 -> 0; matrix products, arithmetic and copies ran while one was open for 6% -> 0% of each run, Pallas kernels for 0% -> 0%
where the time goes in v1:
time: 74.5 us; the launch traced here: 74.2 us
  Pallas kernels  68.6 us (92%)
  local copies, waits for them, and re-layouts  4.6 us (6%)
  other arithmetic  0.92 us (1%)
    pallas_call x1, Pallas kernels, shards(): pl.pallas_call(functools.partial(kernel, n, rows, pad, tile), out_shape=j...  68.6 us
    unnamed x12, local copies, waits for them, and re-layouts  3.16 us

profile of v1, /device:TPU:11, one launch (start us, length us, event | category | flops | bytes accessed | tf_op | source)
XLA Modules:
  0.0 74.2 jit_solution(12188278379564629916)
XLA Ops:
  0.0 0.0 copy-start
  0.0 0.0 copy-start.4
  0.0 0.0 copy-start.5
  0.0 0.8 %select_reduce_fusion = s32[16]{0:T(128)S(1)} fusion(s32[16]{0:T(128)} %param.12), kind=kLoop, calls=%fused_computation.4 | loop fusion | flops 752 | bytes 128 | tf_op jit(solution)/shard_map/reduce_sum | solution.py:298
  0.8 0.0 copy-done.4
  0.8 0.0 copy-done.5
  0.9 0.1 subtract_minimum_fusion.counts
  0.9 0.7 stack.9
  1.7 0.0 copy-start.3
  1.7 0.7 copy-done.3
  2.4 0.0 copy-done
  2.5 0.0 copy-start.1
  2.5 1.2 %copy-done.1 = bf16[1024,512]{1,0:T(8,128)(2,1)S(1)} copy-done((bf16[1024,512]{1,0:T(8,128)(2,1)S(1)}, bf16[1024,512]{1,0:T(8,128)(2,1)}, u32[]{:S(2)}) %copy-start.1) | copy-done | bytes 1048600
  3.7 0.0 copy-start.2
  3.7 1.2 %copy-done.2 = bf16[1024,512]{1,0:T(8,128)(2,1)S(1)} copy-done((bf16[1024,512]{1,0:T(8,128)(2,1)S(1)}, bf16[1024,512]{1,0:T(8,128)(2,1)}, u32[]{:S(2)}) %copy-start.2) | copy-done | bytes 1048600
  4.9 68.6 %spanned_attention.1 = bf16[4,128,128]{2,1,0:T(8,128)(2,1)S(1)} custom-call(s32[16,2]{1,0:T(8,128)S(1)} %subtract_minimum_fusion.counts, bf16[4,128,128]{2,1,0:T(8,128)(2,1)S(1)} %bitcast.18, bf16[4,2,16,128]{3,2,1,0:T(8,128)(2,1)S(1)} %maximum_bitcast_fusion.s_in, bf16[1024,512]{1,0:T(8,128)(2,1)S(1)} %copy-done.1, bf16[1024,512]{1,0:T(8,128)(2,1)S(1)} %copy-done.2), custom_call_target="tpu_custom_call" | custom-call | tf_op jit(solution)/shard_map/spanned_attention/pallas_call | solution.py:305
  73.5 0.7 copy.22
  (5 shorter events, 0.1 us)
Async XLA Ops:
  0.0 2.4 %copy-start = (bf16[16,4096]{1,0:T(8,128)(2,1)S(1)}, bf16[16,4096]{1,0:T(8,128)(2,1)}, u32[]{:S(2)}) copy-start(bf16[16,4096]{1,0:T(8,128)(2,1)} %param.7) | copy-start | bytes 393220
  0.0 0.8 %copy-start.4 = (s32[16]{0:T(128)S(1)}, s32[16]{0:T(128)}, u32[]{:S(2)}) copy-start(s32[16]{0:T(128)} %param.12) | copy-start | bytes 196
  0.0 0.8 %copy-start.5 = (s32[2]{0:T(128)S(1)}, s32[2]{0:T(128)}, u32[]{:S(2)}) copy-start(s32[2]{0:T(128)} %param.13) | copy-start | bytes 28
  1.7 0.7 copy-start.3
  2.5 1.2 %copy-start.1 = (bf16[1024,512]{1,0:T(8,128)(2,1)S(1)}, bf16[1024,512]{1,0:T(8,128)(2,1)}, u32[]{:S(2)}) copy-start(bf16[1024,512]{1,0:T(8,128)(2,1)} %k_in.1) | copy-start | bytes 3145732
  3.7 1.2 %copy-start.2 = (bf16[1024,512]{1,0:T(8,128)(2,1)S(1)}, bf16[1024,512]{1,0:T(8,128)(2,1)}, u32[]{:S(2)}) copy-start(bf16[1024,512]{1,0:T(8,128)(2,1)} %v_in.1) | copy-start | bytes 3145732

commit v2 on v1

--- a/solution.py
+++ b/solution.py
@@ -14,6 +14,8 @@
 SPAN = 128
 SPANS = 2
 NEG = -1e30
+LEVELS = 32767.0
+TINY = 1e-33
 SCALE2 = HEAD_SIZE ** (-0.5) * 1.4426950408889634
 F32 = jnp.float32
 BF16 = jnp.bfloat16
@@ -49,9 +51,9 @@
 
 def kernel(
     n, rows, pad, tile,
-    counts, q_in, s_in, k_in, v_in, out,
-    qbuf, sbuf, kbuf, vbuf, vt, svt, acc, rbuf, obuf,
-    q_send, q_recv, s_send, s_recv, k_send, k_recv, v_send, v_recv, a_send, a_recv, o_send, o_recv,
+    lens, starts, q_in, sk_in, sv_in, k_in, v_in, out,
+    s_in, qbuf, sbuf, kbuf, vbuf, vt, svt, acc, coded, stats, rbuf, rstat, obuf,
+    q_send, q_recv, s_send, s_recv, k_send, k_recv, v_send, v_recv, a_send, a_recv, t_send, t_recv, o_send, o_recv,
 ):
     group = lax.axis_index("groups")
     me = lax.axis_index("kvp")
@@ -64,6 +66,9 @@
     slots = kbuf.shape[1]
 
     barrier = pltpu.get_barrier_semaphore()
+    for h in range(HEADS):
+        for at, ref in enumerate((sk_in, sv_in)):
+            s_in[h, at] = ref[:, h * HEAD_SIZE : (h + 1) * HEAD_SIZE]
 
     def greet(k, c):
         pl.semaphore_signal(barrier, inc=1, device_id=(group, lax.rem(me + k, n)), device_id_type=MESH)
@@ -142,6 +147,13 @@
                 copy.wait_recv()
         vt[i] = jnp.transpose(vbuf[i])
 
+    def offset(j, totals):
+        length = lens[j]
+        return tuple(
+            total + jnp.where(j < quad * HEADS + order[i], length, 0) for i, total in enumerate(totals)
+        )
+
+    offsets = lax.fori_loop(0, n, offset, (jnp.int32(0),) * HEADS)
     slot_ids = lax.broadcasted_iota(jnp.int32, (slots, tile), 0)
     stat_ids = lax.broadcasted_iota(jnp.int32, (8, tile), 0)
 
@@ -149,7 +161,7 @@
         return qbuf[pl.ds(pl.multiple_of(b * tile, tile), tile), :]
 
     def part(i, b):
-        count = counts[quad * HEADS + order[i], lax.div(b * tile, GROUP * SPAN)]
+        count = jnp.minimum(lens[quad * HEADS + order[i]], starts[lax.div(b * tile, GROUP * SPAN)] - offsets[i])
         weights, top, total = weigh(dot_nt(kbuf[i], queries_of(b)), slot_ids < count)
         return dot_nn(vt[i], weights), top, total
 
@@ -180,32 +192,47 @@
 
     lax.fori_loop(0, quads * tiles, second, 0)
     wait_kv(2)
+
+    def third(b, c):
+        store(b, merge(load(acc, b), part(2, b)))
+        return c
+
+    lax.fori_loop(0, quads * tiles, third, 0)
     wait_kv(3)
 
-    def a_copy(k):
+    def a_copies(k):
         to = lax.rem(quad + k, quads)
-        return pltpu.make_async_remote_copy(
-            src_ref=acc.at[pl.ds(to * tiles, tiles)], dst_ref=rbuf.at[k],
-            send_sem=a_send.at[k], recv_sem=a_recv.at[k],
-            device_id=(group, to * HEADS + head), device_id_type=MESH,
-        )
-
-    def finish(to):
-        def one(t, c):
-            b = to * tiles + t
-            state = merge(load(acc, b), part(2, b))
-            store(b, merge(state, part(3, b)))
-            return c
+        return tuple(
+            pltpu.make_async_remote_copy(
+                src_ref=src.at[pl.ds(to * tiles, tiles)], dst_ref=dst.at[k],
+                send_sem=send.at[k], recv_sem=recv.at[k],
+                device_id=(group, to * HEADS + head), device_id_type=MESH,
+            )
+            for src, dst, send, recv in ((coded, rbuf, a_send, a_recv), (stats, rstat, t_send, t_recv))
+        )
+
+    def finish_and_send(k, c):
+        def one(t, c2):
+            b = lax.rem(quad + k, quads) * tiles + t
+            num, top, total = merge(load(acc, b), part(3, b))
+            level = jnp.maximum(jnp.max(jnp.abs(num), axis=0, keepdims=True), TINY)
+            coded[b] = jnp.round(num * (LEVELS / level)).astype(jnp.int32).astype(jnp.int16)
+            stats[b] = jnp.where(stat_ids < 2, top, jnp.where(stat_ids < 4, total, level * (1.0 / LEVELS)))
+            return c2
 
         lax.fori_loop(0, tiles, one, 0)
-
-    def finish_and_send(k, c):
-        finish(lax.rem(quad + k, quads))
-        a_copy(k).start()
+        for copy in a_copies(k):
+            copy.start()
         return c
 
     lax.fori_loop(1, quads, finish_and_send, 0)
-    finish(quad)
+
+    def finish(t, c):
+        b = quad * tiles + t
+        store(b, merge(load(acc, b), part(3, b)))
+        return c
+
+    lax.fori_loop(0, tiles, finish, 0)
 
     def wait_s(k, c):
         s_copy(k).wait_recv()
@@ -231,11 +258,13 @@
     lax.fori_loop(0, tiles, span, 0)
 
     def gather(k, c):
-        a_copy(k).wait_recv()
+        for copy in a_copies(k):
+            copy.wait_recv()
 
         def one(t, c2):
             b = quad * tiles + t
-            store(b, merge(load(acc, b), load(rbuf, k, t)))
+            num = rbuf[k, t].astype(jnp.int32).astype(F32) * rstat[k, t, 4:5]
+            store(b, merge(load(acc, b), (num, rstat[k, t, 0:1], rstat[k, t, 2:3])))
             return c2
 
         lax.fori_loop(0, tiles, one, 0)
@@ -279,7 +308,8 @@
     lax.fori_loop(1, n, drain, 0)
 
     def drain_a(k, c):
-        a_copy(k).wait_send()
+        for copy in a_copies(k):
+            copy.wait_send()
         return c
 
     lax.fori_loop(1, quads, drain_a, 0)
@@ -294,23 +324,22 @@
     quads = n // HEADS
     tile = min(256, HEADS * block)
     tiles = HEADS * block // tile
-    ids = jnp.arange(n, dtype=jnp.int32)
-    offsets = jnp.sum(jnp.where(ids[None, :] < ids[:, None], shard_lens[None, :], 0), axis=1)
-    counts = jnp.minimum(shard_lens[:, None], span_starts[None, :] - offsets[:, None])
     q = queries.reshape(rows, QUERY_HEADS, HEAD_SIZE).transpose(1, 0, 2).reshape(HEADS, block, HEAD_SIZE)
-    both = jnp.stack([span_keys, span_values]).reshape(2, rows, HEADS, HEAD_SIZE).transpose(2, 0, 1, 3)
-    both = jnp.pad(both, ((0, 0), (0, 0), (0, pad - rows), (0, 0)))
+    span_keys, span_values = (
+        jnp.pad(x, ((0, pad - rows), (0, 0))) if pad > rows else x for x in (span_keys, span_values)
+    )
     vmem = pl.BlockSpec(memory_space=pltpu.VMEM)
+    smem, hbm = pl.BlockSpec(memory_space=pltpu.SMEM), pl.BlockSpec(memory_space=pltpu.HBM)
     dma = pltpu.SemaphoreType.DMA
     out = pl.pallas_call(
         functools.partial(kernel, n, rows, pad, tile),
         out_shape=jax.ShapeDtypeStruct((HEADS, block, HEAD_SIZE), BF16),
         in_specs=[
-            pl.BlockSpec(memory_space=pltpu.SMEM), vmem, vmem,
-            pl.BlockSpec(memory_space=pl.ANY), pl.BlockSpec(memory_space=pl.ANY),
+            smem, smem, vmem, vmem, vmem, hbm, hbm,
         ],
         out_specs=vmem,
         scratch_shapes=[
+            pltpu.VMEM((HEADS, 2, pad, HEAD_SIZE), BF16),
             pltpu.VMEM((n * block, HEAD_SIZE), BF16),
             pltpu.VMEM((2, n * pad, HEAD_SIZE), BF16),
             pltpu.VMEM((HEADS, slots, HEAD_SIZE), BF16),
@@ -318,17 +347,20 @@
             pltpu.VMEM((HEADS, HEAD_SIZE, slots), BF16),
             pltpu.VMEM((HEAD_SIZE, n * pad), BF16),
             pltpu.VMEM((quads * tiles, HEAD_SIZE + 8, tile), F32),
-            pltpu.VMEM((quads, tiles, HEAD_SIZE + 8, tile), F32),
+            pltpu.VMEM((quads * tiles, HEAD_SIZE, tile), jnp.int16),
+            pltpu.VMEM((quads * tiles, 8, tile), F32),
+            pltpu.VMEM((quads, tiles, HEAD_SIZE, tile), jnp.int16),
+            pltpu.VMEM((quads, tiles, 8, tile), F32),
             pltpu.VMEM((HEADS * block, HEAD_SIZE), BF16),
             dma((n,)), dma((n,)), dma((n,)), dma((n,)),
             dma((HEADS,)), dma((HEADS,)), dma((HEADS,)), dma((HEADS,)),
-            dma((quads,)), dma((quads,)), dma((HEADS,)), dma((HEADS,)),
+            dma((quads,)), dma((quads,)), dma((quads,)), dma((quads,)), dma((HEADS,)), dma((HEADS,)),
         ],
         compiler_params=pltpu.CompilerParams(
             collective_id=0, has_side_effects=True, vmem_limit_bytes=48 * 1024 * 1024
         ),
         name="spanned_attention",
-    )(counts, q, both, stored_keys, stored_values)
+    )(shard_lens, span_starts, q, span_keys, span_values, stored_keys, stored_values)
     return out.reshape(QUERY_HEADS, rows, HEAD_SIZE).transpose(1, 0, 2).reshape(rows, QUERY_HEADS * HEAD_SIZE)
 
 

time: 74.5 us -> 63.3 us (0.85); the launches traced: 74.2 us -> 62.1 us
  Pallas kernels: 68.6 us -> 57.4 us
  other arithmetic: 0.92 us -> 0 us
    pallas_call x1, Pallas kernels: 68.6 us -> 57.4 us  [shards(): pl.pallas_call(functools.partial(kernel, n, rows, pad, tile), out_shape=j...]
    reduce_sum x1 -> x0, other arithmetic: 0.83 us -> none  [shards(): jnp.sum(jnp.where(ids[None, :] < ids[:, None], shard_lens[None, :], 0), a...]
    unnamed x12 -> x14, local copies, waits for them, and re-layouts: 3.16 us -> 3.99 us
    another operation x4 -> x0, local copies, waits for them, and re-layouts: 0.75 us -> none  [shards(): jnp.stack([span_keys, span_values]).reshape(2, rows, HEADS, HEAD_SIZE)]
where the time goes in v2:
time: 63.3 us; the launch traced here: 62.1 us
  Pallas kernels  57.4 us (91%)
  local copies, waits for them, and re-layouts  4.68 us (7%)
    pallas_call x1, Pallas kernels, shards(): pl.pallas_call(functools.partial(kernel, n, rows, pad, tile), out_shape=j...  57.4 us
    unnamed x14, local copies, waits for them, and re-layouts  3.99 us

profile of v2, /device:TPU:11, one launch (start us, length us, event | category | flops | bytes accessed | tf_op | source)
XLA Modules:
  0.0 62.1 jit_solution(10547176046707759470)
XLA Ops:
  0.0 0.0 copy-start
  0.0 0.0 copy-start.4
  0.0 0.0 copy-start.3
  0.0 0.9 %copy-done = bf16[16,4096]{1,0:T(8,128)(2,1)S(1)} copy-done((bf16[16,4096]{1,0:T(8,128)(2,1)S(1)}, bf16[16,4096]{1,0:T(8,128)(2,1)}, u32[]{:S(2)}) %copy-start) | copy-done | bytes 131096
  0.9 0.0 copy-start.5
  0.9 0.0 copy-start.6
  1.0 0.0 copy-done.4
  1.0 0.0 copy-done.3
  1.0 0.6 copy-done.5
  1.6 0.0 copy-done.6
  1.6 0.0 copy-start.1
  1.6 1.2 %copy-done.1 = bf16[1024,512]{1,0:T(8,128)(2,1)S(1)} copy-done((bf16[1024,512]{1,0:T(8,128)(2,1)S(1)}, bf16[1024,512]{1,0:T(8,128)(2,1)}, u32[]{:S(2)}) %copy-start.1) | copy-done | bytes 1048600
  2.8 0.0 copy-start.2
  2.8 1.2 %copy-done.2 = bf16[1024,512]{1,0:T(8,128)(2,1)S(1)} copy-done((bf16[1024,512]{1,0:T(8,128)(2,1)S(1)}, bf16[1024,512]{1,0:T(8,128)(2,1)}, u32[]{:S(2)}) %copy-start.2) | copy-done | bytes 1048600
  4.1 57.4 %spanned_attention.1 = bf16[4,128,128]{2,1,0:T(8,128)(2,1)S(1)} custom-call(s32[16]{0:T(128)S(1)} %copy-done.5, s32[2]{0:T(128)S(1)} %copy-done.6, bf16[4,128,128]{2,1,0:T(8,128)(2,1)S(1)} %bitcast.16, bf16[16,512]{1,0:T(8,128)(2,1)S(1)} %copy-done.3, bf16[16,512]{1,0:T(8,128)(2,1)S(1)} %copy-done.4, bf16[1024,512]{1,0:T(8,128)(2,1)S(1)} %copy-done.1, ...), custom_call_target="tpu_custom_call" | custom-call | tf_op jit(solution)/shard_map/spanned_attention/pallas_call | solution.py:334
  61.4 0.7 %copy.14 = bf16[32,2,8,128]{3,2,0,1:T(8,128)(2,1)} copy(bf16[32,2,8,128]{3,2,1,0:T(8,128)(2,1)S(1)} %bitcast.15) | data formatting | bytes 262144 | tf_op jit(solution)/shard_map/reshape | solution.py:364
  (1 shorter events, 0.0 us)
Async XLA Ops:
  0.0 0.9 %copy-start = (bf16[16,4096]{1,0:T(8,128)(2,1)S(1)}, bf16[16,4096]{1,0:T(8,128)(2,1)}, u32[]{:S(2)}) copy-start(bf16[16,4096]{1,0:T(8,128)(2,1)} %param.7) | copy-start | bytes 393220
  0.0 1.0 %copy-start.4 = (bf16[16,512]{1,0:T(8,128)(2,1)S(1)}, bf16[16,512]{1,0:T(8,128)(2,1)}, u32[]{:S(2)}) copy-start(bf16[16,512]{1,0:T(8,128)(2,1)} %sv_in.1) | copy-start | bytes 49156
  0.0 1.0 %copy-start.3 = (bf16[16,512]{1,0:T(8,128)(2,1)S(1)}, bf16[16,512]{1,0:T(8,128)(2,1)}, u32[]{:S(2)}) copy-start(bf16[16,512]{1,0:T(8,128)(2,1)} %sk_in.1) | copy-start | bytes 49156
  0.9 0.7 %copy-start.5 = (s32[16]{0:T(128)S(1)}, s32[16]{0:T(128)}, u32[]{:S(2)}) copy-start(s32[16]{0:T(128)} %lens.1) | copy-start | bytes 196
  0.9 0.7 %copy-start.6 = (s32[2]{0:T(128)S(1)}, s32[2]{0:T(128)}, u32[]{:S(2)}) copy-start(s32[2]{0:T(128)} %starts.1) | copy-start | bytes 28
  1.6 1.2 %copy-start.1 = (bf16[1024,512]{1,0:T(8,128)(2,1)S(1)}, bf16[1024,512]{1,0:T(8,128)(2,1)}, u32[]{:S(2)}) copy-start(bf16[1024,512]{1,0:T(8,128)(2,1)} %k_in.1) | copy-start | bytes 3145732
  2.8 1.2 %copy-start.2 = (bf16[1024,512]{1,0:T(8,128)(2,1)S(1)}, bf16[1024,512]{1,0:T(8,128)(2,1)}, u32[]{:S(2)}) copy-start(bf16[1024,512]{1,0:T(8,128)(2,1)} %v_in.1) | copy-start | bytes 3145732

commit v3 on v2

--- a/solution.py
+++ b/solution.py
@@ -133,11 +133,13 @@
     qbuf[pl.ds(pl.multiple_of(me * block, block), block), :] = q_in[head]
     sbuf[:, pl.ds(pl.multiple_of(me * pad, pad), pad), :] = s_in[head]
 
-    def wait_q(k, c):
-        q_copy(k).wait_recv()
-        return c
-
-    lax.fori_loop(1, n, wait_q, 0)
+    def wait_q(b):
+        for j in range(tile // block):
+            k = lax.rem(me + n - (b * (tile // block) + j), n)
+
+            @pl.when(k > 0)
+            def _():
+                q_copy(k).wait_recv()
 
     def wait_kv(i):
         for copy in kv[i]:
@@ -178,26 +180,22 @@
         acc[b, HEAD_SIZE : HEAD_SIZE + 8] = jnp.where(stat_ids < 4, top, total)
 
     wait_kv(0)
-
-    def first(b, c):
-        store(b, part(0, b))
+    wait_kv(1)
+
+    def first(u, c):
+        b = lax.rem(quad * tiles + u, quads * tiles)
+        wait_q(b)
+        store(b, merge(part(0, b), part(1, b)))
         return c
 
     lax.fori_loop(0, quads * tiles, first, 0)
-    wait_kv(1)
-
-    def second(b, c):
-        store(b, merge(load(acc, b), part(1, b)))
-        return c
-
-    lax.fori_loop(0, quads * tiles, second, 0)
     wait_kv(2)
 
     def third(b, c):
         store(b, merge(load(acc, b), part(2, b)))
         return c
 
-    lax.fori_loop(0, quads * tiles, third, 0)
+    lax.fori_loop(0, quads * tiles, third, 0, unroll=2)
     wait_kv(3)
 
     def a_copies(k):
@@ -220,7 +218,7 @@
             stats[b] = jnp.where(stat_ids < 2, top, jnp.where(stat_ids < 4, total, level * (1.0 / LEVELS)))
             return c2
 
-        lax.fori_loop(0, tiles, one, 0)
+        lax.fori_loop(0, tiles, one, 0, unroll=tiles)
         for copy in a_copies(k):
             copy.start()
         return c
@@ -232,7 +230,7 @@
         store(b, merge(load(acc, b), part(3, b)))
         return c
 
-    lax.fori_loop(0, tiles, finish, 0)
+    lax.fori_loop(0, tiles, finish, 0, unroll=tiles)
 
     def wait_s(k, c):
         s_copy(k).wait_recv()
@@ -255,7 +253,7 @@
         store(b, merge(load(acc, b), (dot_nn(svt[...], weights), top, total)))
         return c
 
-    lax.fori_loop(0, tiles, span, 0)
+    lax.fori_loop(0, tiles, span, 0, unroll=tiles)
 
     def gather(k, c):
         for copy in a_copies(k):
@@ -277,7 +275,7 @@
         obuf[pl.ds(pl.multiple_of(t * tile, tile), tile), :] = jnp.transpose(num / total).astype(BF16)
         return c
 
-    lax.fori_loop(0, tiles, normal, 0)
+    lax.fori_loop(0, tiles, normal, 0, unroll=tiles)
 
     def o_copy(i):
         return pltpu.make_async_remote_copy(
@@ -322,7 +320,7 @@
     pad = max(rows, 16)
     block = GROUP * rows
     quads = n // HEADS
-    tile = min(256, HEADS * block)
+    tile = min(512, HEADS * block)
     tiles = HEADS * block // tile
     q = queries.reshape(rows, QUERY_HEADS, HEAD_SIZE).transpose(1, 0, 2).reshape(HEADS, block, HEAD_SIZE)
     span_keys, span_values = (
@@ -357,7 +355,7 @@
             dma((quads,)), dma((quads,)), dma((quads,)), dma((quads,)), dma((HEADS,)), dma((HEADS,)),
         ],
         compiler_params=pltpu.CompilerParams(
-            collective_id=0, has_side_effects=True, vmem_limit_bytes=48 * 1024 * 1024
+            collective_id=0, has_side_effects=True, vmem_limit_bytes=62 * 1024 * 1024
         ),
         name="spanned_attention",
     )(shard_lens, span_starts, q, span_keys, span_values, stored_keys, stored_values)

time: 63.3 us -> 59.7 us (0.943); the launches traced: 62.1 us -> 59.5 us
  local copies, waits for them, and re-layouts: 4.68 us -> 3.16 us
  Pallas kernels: 57.4 us -> 56.4 us
    unnamed x14 -> x2, local copies, waits for them, and re-layouts: 3.99 us -> 0.9 us
    pallas_call x1, Pallas kernels: 57.4 us -> 56.4 us  [shards(): pl.pallas_call(functools.partial(kernel, n, rows, pad, tile), out_shape=j...]
    reshape x1, local copies, waits for them, and re-layouts: 0.67 us -> 1.58 us  [shards(): out.reshape(QUERY_HEADS, rows, HEAD_SIZE).transpose(1, 0, 2)]
    reshape x1, local copies, waits for them, and re-layouts: 0.02 us -> 0.68 us  [shards(): queries.reshape(rows, QUERY_HEADS, HEAD_SIZE).transpose(1, 0, 2)]
where the time goes in v3:
time: 59.7 us; the launch traced here: 59.5 us
  Pallas kernels  56.4 us (94%)
  local copies, waits for them, and re-layouts  3.16 us (5%)
    pallas_call x1, Pallas kernels, shards(): pl.pallas_call(functools.partial(kernel, n, rows, pad, tile), out_shape=j...  56.4 us
    reshape x1, local copies, waits for them, and re-layouts, shards(): out.reshape(QUERY_HEADS, rows, HEAD_SIZE).transpose(1, 0, 2)  1.58 us

profile of v3, /device:TPU:11, one launch (start us, length us, event | category | flops | bytes accessed | tf_op | source)
XLA Modules:
  0.0 59.5 jit_solution(14126942611469142694)
XLA Ops:
  0.0 0.0 copy-start
  0.0 0.9 %copy-done = bf16[16,4096]{1,0:T(8,128)(2,1)S(1)} copy-done((bf16[16,4096]{1,0:T(8,128)(2,1)S(1)}, bf16[16,4096]{1,0:T(8,128)(2,1)}, u32[]{:S(2)}) %copy-start) | copy-done | bytes 131096
  0.9 0.7 %copy_bitcast_fusion.1 = bf16[16,32,128]{2,0,1:T(8,128)(2,1)} fusion(bf16[16,4096]{1,0:T(8,128)(2,1)S(1)} %copy-done), kind=kLoop, calls=%fused_computation.1 | loop fusion | bytes 262144 | tf_op jit(solution)/shard_map/reshape | solution.py:325
  1.6 56.4 %spanned_attention.1 = bf16[4,128,128]{2,1,0:T(8,128)(2,1)} custom-call(s32[16]{0:T(128)} %lens.1, s32[2]{0:T(128)} %starts.1, bf16[4,128,128]{2,1,0:T(8,128)(2,1)} %bitcast.16, bf16[16,512]{1,0:T(8,128)(2,1)} %sk_in.1, bf16[16,512]{1,0:T(8,128)(2,1)} %sv_in.1, bf16[1024,512]{1,0:T(8,128)(2,1)} %k_in.1, bf16[1024,512]{1,0:T(8,128)(2,1)} %v_in.1), custom_call_target="tpu_custom_call" | custom-call | tf_op jit(solution)/shard_map/spanned_attention/pallas_call | solution.py:332
  57.9 1.6 %copy.14 = bf16[32,2,8,128]{3,2,0,1:T(8,128)(2,1)} copy(bf16[32,2,8,128]{3,2,1,0:T(8,128)(2,1)} %bitcast.15) | data formatting | bytes 262144 | tf_op jit(solution)/shard_map/reshape | solution.py:362
Async XLA Ops:
  0.0 0.9 %copy-start = (bf16[16,4096]{1,0:T(8,128)(2,1)S(1)}, bf16[16,4096]{1,0:T(8,128)(2,1)}, u32[]{:S(2)}) copy-start(bf16[16,4096]{1,0:T(8,128)(2,1)} %param.7) | copy-start | bytes 393220

commit v4 on v3

--- a/solution.py
+++ b/solution.py
@@ -26,8 +26,7 @@
     return x.bit_length() - 1
 
 
-def weigh(scores, visible):
-    masked = jnp.where(visible, scores, NEG)
+def weigh(masked):
     top = jnp.max(masked, axis=0, keepdims=True)
     weights = jnp.exp2(masked * SCALE2 - top * SCALE2)
     return weights.astype(BF16), top * SCALE2, jnp.sum(weights, axis=0, keepdims=True)
@@ -156,7 +155,8 @@
         )
 
     offsets = lax.fori_loop(0, n, offset, (jnp.int32(0),) * HEADS)
-    slot_ids = lax.broadcasted_iota(jnp.int32, (slots, tile), 0)
+    lanes = min(tile, 128)
+    slot_ids = lax.broadcasted_iota(jnp.int32, (slots, lanes), 0)
     stat_ids = lax.broadcasted_iota(jnp.int32, (8, tile), 0)
 
     def queries_of(b):
@@ -164,7 +164,8 @@
 
     def part(i, b):
         count = jnp.minimum(lens[quad * HEADS + order[i]], starts[lax.div(b * tile, GROUP * SPAN)] - offsets[i])
-        weights, top, total = weigh(dot_nt(kbuf[i], queries_of(b)), slot_ids < count)
+        bias = jnp.where(slot_ids < count, 0.0, NEG).astype(F32)
+        weights, top, total = weigh(dot_nt(kbuf[i], queries_of(b)) + jnp.concatenate([bias] * (tile // lanes), axis=1))
         return dot_nn(vt[i], weights), top, total
 
     def load(ref, *at):
@@ -249,7 +250,7 @@
         ids = lane_ids + b * tile
         q_rows = (ids >> log2(block)) * rows + (ids & (rows - 1))
         visible = key_live & (key_rows >> log2(SPAN) == q_rows >> log2(SPAN)) & (key_rows <= q_rows)
-        weights, top, total = weigh(dot_nt(sbuf[0], queries_of(b)), visible)
+        weights, top, total = weigh(jnp.where(visible, dot_nt(sbuf[0], queries_of(b)), NEG))
         store(b, merge(load(acc, b), (dot_nn(svt[...], weights), top, total)))
         return c
 

time: 59.7 us -> 59.7 us (level)
  no operation moved by 1% of the time
where the time goes in v4:
time: 59.7 us; the launch traced here: 59.5 us
  Pallas kernels  56.4 us (94%)
  local copies, waits for them, and re-layouts  3.16 us (5%)
    pallas_call x1, Pallas kernels, shards(): pl.pallas_call(functools.partial(kernel, n, rows, pad, tile), out_shape=j...  56.4 us
    reshape x1, local copies, waits for them, and re-layouts, shards(): out.reshape(QUERY_HEADS, rows, HEAD_SIZE).transpose(1, 0, 2)  1.58 us

profile of v4, /device:TPU:11, one launch (start us, length us, event | category | flops | bytes accessed | tf_op | source)
XLA Modules:
  0.0 59.5 jit_solution(14391449120603811854)
XLA Ops:
  0.0 0.0 copy-start
  0.0 0.9 %copy-done = bf16[16,4096]{1,0:T(8,128)(2,1)S(1)} copy-done((bf16[16,4096]{1,0:T(8,128)(2,1)S(1)}, bf16[16,4096]{1,0:T(8,128)(2,1)}, u32[]{:S(2)}) %copy-start) | copy-done | bytes 131096
  0.9 0.7 %copy_bitcast_fusion.1 = bf16[16,32,128]{2,0,1:T(8,128)(2,1)} fusion(bf16[16,4096]{1,0:T(8,128)(2,1)S(1)} %copy-done), kind=kLoop, calls=%fused_computation.1 | loop fusion | bytes 262144 | tf_op jit(solution)/shard_map/reshape | solution.py:326
  1.6 56.4 %spanned_attention.1 = bf16[4,128,128]{2,1,0:T(8,128)(2,1)} custom-call(s32[16]{0:T(128)} %lens.1, s32[2]{0:T(128)} %starts.1, bf16[4,128,128]{2,1,0:T(8,128)(2,1)} %bitcast.16, bf16[16,512]{1,0:T(8,128)(2,1)} %sk_in.1, bf16[16,512]{1,0:T(8,128)(2,1)} %sv_in.1, bf16[1024,512]{1,0:T(8,128)(2,1)} %k_in.1, bf16[1024,512]{1,0:T(8,128)(2,1)} %v_in.1), custom_call_target="tpu_custom_call" | custom-call | tf_op jit(solution)/shard_map/spanned_attention/pallas_call | solution.py:333
  58.0 1.6 %copy.14 = bf16[32,2,8,128]{3,2,0,1:T(8,128)(2,1)} copy(bf16[32,2,8,128]{3,2,1,0:T(8,128)(2,1)} %bitcast.15) | data formatting | bytes 262144 | tf_op jit(solution)/shard_map/reshape | solution.py:363
Async XLA Ops:
  0.0 0.9 %copy-start = (bf16[16,4096]{1,0:T(8,128)(2,1)S(1)}, bf16[16,4096]{1,0:T(8,128)(2,1)}, u32[]{:S(2)}) copy-start(bf16[16,4096]{1,0:T(8,128)(2,1)} %param.7) | copy-start | bytes 393220
